TPU v7x, 32 devices: a whole 2x2x4 slice. The times are simulated.
32 devices in a mesh: dp: 8 (over y, x, core), mp: 4 (over z).
Axes of the slice: x: 2, y: 2, z: 4, core: 2. Of those that a mesh axis runs over, the one named last changes fastest.
Arguments:
- frames: bfloat16 [11008, 768], P(('dp', 'mp')), may hold values from -6 to 6
- span_mask: int32 [16, 688], P('dp'), may hold values from 0 to 1, as said below
- cotangent: bfloat16 [11008, 768], P(('dp', 'mp')), may hold values from -6 to 6
- qkv_weight: float32 [768, 2304], P('dp', 'mp'), may hold values from -0.21875 to 0.21875
- qkv_mean: float32 [768, 2304], P('dp', 'mp'), may hold values from -0.00061035156 to 0.00061035156
- qkv_square: float32 [768, 2304], P('dp', 'mp'), may hold values from 7.064254e-11 to 1.1302806e-09
- out_weight: float32 [768, 768], P('mp', 'dp'), may hold values from -3.5 to 3.5
- out_mean: float32 [768, 768], P('mp', 'dp'), may hold values from -0.00061035156 to 0.00061035156
- out_square: float32 [768, 768], P('mp', 'dp'), may hold values from 2.8257017e-12 to 4.2385526e-11
- up_weight: float32 [768, 3072], P('dp', 'mp'), may hold values from -0.21875 to 0.21875
- up_mean: float32 [768, 3072], P('dp', 'mp'), may hold values from -0.00061035156 to 0.00061035156
- up_square: float32 [768, 3072], P('dp', 'mp'), may hold values from 7.064254e-11 to 1.1302806e-09
- down_weight: float32 [3072, 768], P('mp', 'dp'), may hold values from -0.109375 to 0.109375
- down_mean: float32 [3072, 768], P('mp', 'dp'), may hold values from -0.00061035156 to 0.00061035156
- down_square: float32 [3072, 768], P('mp', 'dp'), may hold values from 7.064254e-11 to 1.1302806e-09
- head_biases: float32 [12, 384], P('mp', 'dp'), may hold values from -4 to 4
- bias_mean: float32 [12, 384], P('mp', 'dp'), may hold values from -0.00061035156 to 0.00061035156
- bias_square: float32 [12, 384], P('mp', 'dp'), may hold values from 7.064254e-11 to 1.1302806e-09
- norm_vectors: float32 [7, 768], P(None, 'dp'), may hold values from -4 to 4
- vector_mean: float32 [7, 768], P(None, 'dp'), may hold values from -0.00061035156 to 0.00061035156
- vector_square: float32 [7, 768], P(None, 'dp'), may hold values from 7.064254e-11 to 1.1302806e-09
Outputs:
- activations: float32 [11008, 768], P(('dp', 'mp'))
- frame_grad: float32 [11008, 768], P(('dp', 'mp'))
- grad_norm: float32 [], replicated
- qkv_master: float32 [768, 2304], P('dp', 'mp')
- qkv_moment: float32 [768, 2304], P('dp', 'mp')
- qkv_variance: float32 [768, 2304], P('dp', 'mp')
- out_master: float32 [768, 768], P('mp', 'dp')
- out_moment: float32 [768, 768], P('mp', 'dp')
- out_variance: float32 [768, 768], P('mp', 'dp')
- up_master: float32 [768, 3072], P('dp', 'mp')
- up_moment: float32 [768, 3072], P('dp', 'mp')
- up_variance: float32 [768, 3072], P('dp', 'mp')
- down_master: float32 [3072, 768], P('mp', 'dp')
- down_moment: float32 [3072, 768], P('mp', 'dp')
- down_variance: float32 [3072, 768], P('mp', 'dp')
- bias_master: float32 [12, 384], P('mp', 'dp')
- bias_moment: float32 [12, 384], P('mp', 'dp')
- bias_variance: float32 [12, 384], P('mp', 'dp')
- vector_master: float32 [7, 768], P(None, 'dp')
- vector_moment: float32 [7, 768], P(None, 'dp')
- vector_variance: float32 [7, 768], P(None, 'dp')
Inputs may be any that keep to these rules, and one draw needn't show every extreme that they name: `span_mask`: masked frames come in spans of 10 consecutive frames begun at random frames of a clip (spans may join or be cut by the clip's end); the share of masked frames differs from clip to clip.
All inputs are finite; a program needn't handle non-finite values.
Results may differ from a plain program's by a relative error of at most 0.017.
Values may be sent and summed in bfloat16 or wider, within the bound.
A program may use at most 128 MiB of HBM per device.

v0:
```python
import jax
import jax.numpy as jnp
from jax import lax
from jax.sharding import PartitionSpec as P

HD = 64
LEN = 688
norm_eps = 1e-05
adam_eps = 1e-08
beta_one = 0.9
beta_two = 0.999
step_count = 10.0
clip_limit = 1.0
settings = ((0.05, 0.1), (0.3, 0.1), (0.05, 0.1), (0.03, 0.1), (0.3, 0.0), (0.4, 0.0))


def norm_rows(values, norm_gain, norm_shift):
    centred = values - jnp.mean(values, axis=-1, keepdims=True)
    variance = jnp.mean(centred * centred, axis=-1, keepdims=True)
    inverse = lax.rsqrt(variance + norm_eps)
    normed = centred * inverse
    return (normed * norm_gain + norm_shift, normed, inverse)


def norm_back(upstream, normed, inverse, norm_gain):
    scaled = upstream * norm_gain
    inner_part = (
        scaled
        - jnp.mean(scaled, axis=-1, keepdims=True)
        - normed * jnp.mean(scaled * normed, axis=-1, keepdims=True)
    )
    return (inverse * inner_part, jnp.sum(upstream * normed, axis=0), jnp.sum(upstream, axis=0))


def gelu_slope(pre_act):
    cumulative = 0.5 * (1.0 + jax.scipy.special.erf(pre_act * 0.7071067811865476))
    return cumulative + pre_act * jnp.exp(-0.5 * pre_act * pre_act) * 0.3989422804014327


def attend_forward(clip_block):
    scaling = HD ** (-0.5)
    queries = clip_block[:, :, 0]
    key_rows = clip_block[:, :, 1]
    value_rows = clip_block[:, :, 2]
    scores = (
        jnp.einsum("qhe,khe->hqk", queries, key_rows, preferred_element_type=jnp.float32) * scaling
    )
    row_peak = jnp.max(scores, axis=-1, keepdims=True)
    log_total = row_peak + jnp.log(jnp.sum(jnp.exp(scores - row_peak), axis=-1, keepdims=True))
    attention = jnp.exp(scores - log_total).astype(jnp.bfloat16)
    mixed_rows = jnp.einsum(
        "hqk,khe->qhe", attention, value_rows, preferred_element_type=jnp.float32
    )
    return (mixed_rows.astype(jnp.bfloat16).reshape(clip_block.shape[0], -1), log_total)


def attend_backward(pieces):
    clip_block, log_total, grad_mixed = pieces
    scaling = HD ** (-0.5)
    queries = clip_block[:, :, 0]
    key_rows = clip_block[:, :, 1]
    value_rows = clip_block[:, :, 2]
    scores = (
        jnp.einsum("qhe,khe->hqk", queries, key_rows, preferred_element_type=jnp.float32) * scaling
    )
    attention = jnp.exp(scores - log_total)
    attention_low = attention.astype(jnp.bfloat16)
    mixed_rows = jnp.einsum(
        "hqk,khe->qhe", attention_low, value_rows, preferred_element_type=jnp.float32
    ).astype(jnp.bfloat16)
    grad_rows = grad_mixed.reshape(queries.shape)
    grad_attention = jnp.einsum(
        "qhe,khe->hqk", grad_rows, value_rows, preferred_element_type=jnp.float32
    )
    grad_values = jnp.einsum(
        "hqk,qhe->khe", attention_low, grad_rows, preferred_element_type=jnp.float32
    )
    row_inner = jnp.sum(attention * grad_attention, axis=-1, keepdims=True)
    grad_scores = (attention * (grad_attention - row_inner)).astype(jnp.bfloat16)
    grad_queries = (
        jnp.einsum("hqk,khe->qhe", grad_scores, key_rows, preferred_element_type=jnp.float32)
        * scaling
    )
    grad_keys = (
        jnp.einsum("hqk,qhe->khe", grad_scores, queries, preferred_element_type=jnp.float32)
        * scaling
    )
    grad_block = jnp.stack([grad_queries, grad_keys, grad_values], axis=2).astype(jnp.bfloat16)
    return (
        mixed_rows.reshape(clip_block.shape[0], -1),
        grad_block.reshape(clip_block.shape[0], -1),
    )


def adam_step(weight, mean_old, square_old, gradient, factor, rate, decay):
    clipped = gradient * factor
    mean_new = beta_one * mean_old + (1.0 - beta_one) * clipped
    square_new = beta_two * square_old + (1.0 - beta_two) * clipped * clipped
    mean_hat = mean_new / (1.0 - beta_one**step_count)
    square_hat = square_new / (1.0 - beta_two**step_count)
    weight_new = weight - rate * (mean_hat / (jnp.sqrt(square_hat) + adam_eps) + decay * weight)
    return (weight_new, mean_new, square_new)


def on_device(
    frames,
    span_mask,
    cotangent,
    qkv_weight,
    qkv_mean,
    qkv_square,
    out_weight,
    out_mean,
    out_square,
    up_weight,
    up_mean,
    up_square,
    down_weight,
    down_mean,
    down_square,
    head_biases,
    bias_mean,
    bias_square,
    norm_vectors,
    vector_mean,
    vector_square,
):
    masters = (qkv_weight, out_weight, up_weight, down_weight, head_biases, norm_vectors)
    lowered = tuple((weight.astype(jnp.bfloat16) for weight in masters))
    qkv_full, out_full, up_full, down_full, bias_full, vector_full = (
        lax.all_gather(lowered[0], "dp", axis=0, tiled=True),
        lax.all_gather(lowered[1], "dp", axis=1, tiled=True),
        lax.all_gather(lowered[2], "dp", axis=0, tiled=True),
        lax.all_gather(lowered[3], "dp", axis=1, tiled=True),
        lax.all_gather(lowered[4], "dp", axis=1, tiled=True),
        lax.all_gather(lowered[5], "dp", axis=1, tiled=True),
    )
    share_rows = frames.shape[0]
    start_row = lax.axis_index("mp") * share_rows
    vectors = vector_full.astype(jnp.float32)
    local_heads = bias_full.shape[0]

    def share_of(array_full):
        return lax.dynamic_slice_in_dim(array_full, start_row, share_rows, 0)

    gathered = lax.all_gather(frames, "mp", axis=0, tiled=True)
    all_rows = gathered.shape[0]
    masked = span_mask.reshape(all_rows, 1) == 1
    inputs = jnp.where(masked, vectors[0], gathered.astype(jnp.float32))
    rounded = inputs.astype(jnp.bfloat16)
    zero_bias = jnp.zeros_like(bias_full[:, :HD])
    qkv_bias = (
        jnp.stack([bias_full[:, :HD], zero_bias, bias_full[:, HD : 2 * HD]], axis=1)
        .reshape(-1)
        .astype(jnp.float32)
    )
    up_bias = bias_full[:, 2 * HD :].reshape(-1).astype(jnp.float32)
    projected = (jnp.dot(rounded, qkv_full, preferred_element_type=jnp.float32) + qkv_bias).astype(
        jnp.bfloat16
    )
    blocks = projected.reshape(-1, LEN, local_heads, 3, HD)
    mixed_rows, log_total = lax.map(attend_forward, blocks)
    mixed_rows = mixed_rows.reshape(all_rows, -1)
    attn_part = jnp.dot(mixed_rows, out_full, preferred_element_type=jnp.float32)
    attended = lax.psum(attn_part, "mp")
    first_sum = inputs + attended + vectors[5]
    hidden, normed_full, inverse_full = norm_rows(first_sum, vectors[1], vectors[2])
    normed_one = share_of(normed_full)
    inverse_one = share_of(inverse_full)
    hidden_low = hidden.astype(jnp.bfloat16)
    pre_act = jnp.dot(hidden_low, up_full, preferred_element_type=jnp.float32) + up_bias
    activated = jax.nn.gelu(pre_act, approximate=False).astype(jnp.bfloat16)
    ffn_part = jnp.dot(activated, down_full, preferred_element_type=jnp.float32)
    second_sum = hidden + lax.psum(ffn_part, "mp") + vectors[6]
    outputs_full, normed_full, inverse_full = norm_rows(second_sum, vectors[3], vectors[4])
    outputs = share_of(outputs_full)
    normed_two = share_of(normed_full)
    inverse_two = share_of(inverse_full)
    qkv_full, out_full, up_full, down_full, bias_full, vector_full = (
        lax.all_gather(lowered[0], "dp", axis=0, tiled=True),
        lax.all_gather(lowered[1], "dp", axis=1, tiled=True),
        lax.all_gather(lowered[2], "dp", axis=0, tiled=True),
        lax.all_gather(lowered[3], "dp", axis=1, tiled=True),
        lax.all_gather(lowered[4], "dp", axis=1, tiled=True),
        lax.all_gather(lowered[5], "dp", axis=1, tiled=True),
    )
    upstream = cotangent.astype(jnp.float32)
    grad_two, grad_gain_two, grad_shift_two = norm_back(
        upstream, normed_two, inverse_two, vectors[3]
    )
    grad_down_bias = jnp.sum(grad_two, axis=0)
    grad_two_full = lax.all_gather(grad_two.astype(jnp.bfloat16), "mp", axis=0, tiled=True)
    pre_again = jnp.dot(hidden_low, up_full, preferred_element_type=jnp.float32) + up_bias
    act_again = jax.nn.gelu(pre_again, approximate=False).astype(jnp.bfloat16)
    grad_down = jnp.einsum(
        "tf,td->fd", act_again, grad_two_full, preferred_element_type=jnp.float32
    )
    grad_act = jnp.einsum("td,fd->tf", grad_two_full, down_full, preferred_element_type=jnp.float32)
    grad_pre = (grad_act * gelu_slope(pre_again)).astype(jnp.bfloat16)
    grad_up = jnp.einsum("td,tf->df", hidden_low, grad_pre, preferred_element_type=jnp.float32)
    grad_up_bias = jnp.sum(grad_pre, axis=0, dtype=jnp.float32)
    hidden_part = jnp.einsum("tf,df->td", grad_pre, up_full, preferred_element_type=jnp.float32)
    grad_hidden = grad_two + lax.psum_scatter(hidden_part, "mp", scatter_dimension=0, tiled=True)
    grad_one, grad_gain_one, grad_shift_one = norm_back(
        grad_hidden, normed_one, inverse_one, vectors[1]
    )
    grad_out_bias = jnp.sum(grad_one, axis=0)
    grad_one_full = lax.all_gather(grad_one.astype(jnp.bfloat16), "mp", axis=0, tiled=True)
    grad_mixed = jnp.einsum(
        "td,cd->tc", grad_one_full, out_full, preferred_element_type=jnp.float32
    ).astype(jnp.bfloat16)
    mixed_again, grad_blocks = lax.map(
        attend_backward, (blocks, log_total, grad_mixed.reshape(-1, LEN, grad_mixed.shape[1]))
    )
    mixed_again = mixed_again.reshape(all_rows, -1)
    grad_blocks = grad_blocks.reshape(all_rows, -1)
    grad_out = jnp.einsum(
        "tc,td->cd", mixed_again, grad_one_full, preferred_element_type=jnp.float32
    )
    grad_qkv = jnp.einsum("td,tc->dc", rounded, grad_blocks, preferred_element_type=jnp.float32)
    bias_sums = jnp.sum(grad_blocks, axis=0, dtype=jnp.float32).reshape(local_heads, 3, HD)
    grad_biases = jnp.concatenate(
        [bias_sums[:, 0], bias_sums[:, 2], grad_up_bias.reshape(local_heads, -1)], axis=1
    )
    input_part = jnp.einsum("tc,dc->td", grad_blocks, qkv_full, preferred_element_type=jnp.float32)
    grad_inputs = grad_one + lax.psum_scatter(
        input_part.astype(jnp.bfloat16), "mp", scatter_dimension=0, tiled=True
    ).astype(jnp.float32)
    masked_share = share_of(masked)
    grad_embed = jnp.sum(jnp.where(masked_share, grad_inputs, 0.0), axis=0)
    frame_grad = jnp.where(masked_share, 0.0, grad_inputs)
    grad_vectors = jnp.stack(
        [
            grad_embed,
            grad_gain_one,
            grad_shift_one,
            grad_gain_two,
            grad_shift_two,
            grad_out_bias,
            grad_down_bias,
        ]
    )
    reduced = (
        lax.psum_scatter(grad_qkv, "dp", scatter_dimension=0, tiled=True),
        lax.psum_scatter(grad_out, "dp", scatter_dimension=1, tiled=True),
        lax.psum_scatter(grad_up, "dp", scatter_dimension=0, tiled=True),
        lax.psum_scatter(grad_down, "dp", scatter_dimension=1, tiled=True),
        lax.psum_scatter(grad_biases, "dp", scatter_dimension=1, tiled=True),
    )
    local_squares = jnp.float32(0.0)
    for portion in reduced:
        local_squares = local_squares + jnp.sum(portion * portion)
    total_squares, vector_total = lax.psum((local_squares, grad_vectors), ("dp", "mp"))
    grad_norm = jnp.sqrt(total_squares + jnp.sum(vector_total * vector_total))
    column_count = norm_vectors.shape[1]
    vector_grad = lax.dynamic_slice_in_dim(
        vector_total, lax.axis_index("dp") * column_count, column_count, 1
    )
    factor = jnp.minimum(1.0, clip_limit / (grad_norm + 1e-06))
    gradients = (reduced[0], reduced[1], reduced[2], reduced[3], reduced[4], vector_grad)
    means = (qkv_mean, out_mean, up_mean, down_mean, bias_mean, vector_mean)
    squares = (qkv_square, out_square, up_square, down_square, bias_square, vector_square)
    updated = []
    for index_at in range(6):
        updated.extend(
            adam_step(
                masters[index_at],
                means[index_at],
                squares[index_at],
                gradients[index_at],
                factor,
                settings[index_at][0],
                settings[index_at][1],
            )
        )
    return (
        outputs,
        frame_grad,
        grad_norm,
        updated[0],
        updated[1],
        updated[2],
        updated[3],
        updated[4],
        updated[5],
        updated[6],
        updated[7],
        updated[8],
        updated[9],
        updated[10],
        updated[11],
        updated[12],
        updated[13],
        updated[14],
        updated[15],
        updated[16],
        updated[17],
    )


def solution(mesh):
    return jax.shard_map(
        on_device,
        mesh=mesh,
        in_specs=(
            P(("dp", "mp"), None),
            P("dp", None),
            P(("dp", "mp"), None),
            P("dp", "mp"),
            P("dp", "mp"),
            P("dp", "mp"),
            P("mp", "dp"),
            P("mp", "dp"),
            P("mp", "dp"),
            P("dp", "mp"),
            P("dp", "mp"),
            P("dp", "mp"),
            P("mp", "dp"),
            P("mp", "dp"),
            P("mp", "dp"),
            P("mp", "dp"),
            P("mp", "dp"),
            P("mp", "dp"),
            P(None, "dp"),
            P(None, "dp"),
            P(None, "dp"),
        ),
        out_specs=(
            P(("dp", "mp"), None),
            P(("dp", "mp"), None),
            P(),
            P("dp", "mp"),
            P("dp", "mp"),
            P("dp", "mp"),
            P("mp", "dp"),
            P("mp", "dp"),
            P("mp", "dp"),
            P("dp", "mp"),
            P("dp", "mp"),
            P("dp", "mp"),
            P("mp", "dp"),
            P("mp", "dp"),
            P("mp", "dp"),
            P("mp", "dp"),
            P("mp", "dp"),
            P("mp", "dp"),
            P(None, "dp"),
            P(None, "dp"),
            P(None, "dp"),
        ),
        check_vma=False,
    )
```

profile of v0, /device:TPU:0, one launch (start us, length us, event | category | flops | bytes accessed | tf_op | source)
XLA Modules:
  0.0 884.5 jit_solution(6685718186284344518)
XLA Ops:
  10.3 10.3 %all-gather.1 = bf16[8,48,3]{1,2,0:T(4,128)(2,1)S(1)} all-gather(bf16[1,48,3]{1,2,0:T(4,128)(2,1)S(1)} %convert_bitcast_fusion.1), channel_id=1, replica_groups=mesh['dp'=8,'mp'=4] {'dp'}, dimensions={0}, use_global_device_ids=true | all-gather | bytes 2592 | tf_op jit(solution)/shard_map/all_gather | solution.py:135
  22.2 8.9 %all-gather = bf16[8,96,7]{1,2,0:T(8,128)(2,1)S(1)} all-gather(bf16[1,96,7]{1,2,0:T(8,128)(2,1)S(1)} %convert_bitcast_fusion), channel_id=1, replica_groups=mesh['dp'=8,'mp'=4] {'dp'}, dimensions={0}, use_global_device_ids=true | all-gather | bytes 12096 | tf_op jit(solution)/shard_map/all_gather | solution.py:136
  33.1 9.6 %all_gather.35 = bf16[192,768]{0,1:T(8,128)(2,1)} all-gather(bf16[192,96]{0,1:T(8,128)(2,1)S(1)} %copy.106), channel_id=1, replica_groups=mesh['dp'=8,'mp'=4] {'dp'}, dimensions={1}, use_global_device_ids=true | all-gather | bytes 331776 | tf_op jit(solution)/shard_map/all_gather | solution.py:132
  43.4 11.0 %all_gather.33 = bf16[768,576]{1,0:T(8,128)(2,1)S(1)} all-gather(bf16[96,576]{1,0:T(8,128)(2,1)S(1)} %convert_element_type.121), channel_id=1, replica_groups=mesh['dp'=8,'mp'=4] {'dp'}, dimensions={0}, use_global_device_ids=true | all-gather | bytes 995328 | tf_op jit(solution)/shard_map/all_gather | solution.py:131
  54.4 4.8 all-gather.8.cloned.1.call-done
  59.2 3.3 fusion.36
  62.5 2.1 reshape.215
  65.0 7.0 while.24
  66.1 1.1 exponential_reduce_fusion.2
  67.3 1.1 fusion.110
  69.6 1.1 exponential_reduce_fusion.2
  70.8 1.1 fusion.110
  71.9 1.4 copy.105
  73.4 2.1 reshape.216
  75.5 2.8 fusion.71
  80.9 152.6 %all-reduce.4.cloned.1.call-done = f32[1376,768]{1,0:T(8,128)} async-done(((f32[1376,768]{1,0:T(8,128)}), f32[1376,768]{1,0:T(8,128)}) %all-reduce.4.cloned.1.call-update) | async-done | bytes 4227088 | tf_op jit(solution)/shard_map/psum | solution.py:165
  233.5 4.0 fusion.58
  238.3 1.3 multiply_reduce_fusion.3
  239.6 2.6 subtract_multiply_fusion.1
  242.2 13.6 %fusion.20 = (bf16[1376,768]{1,0:T(8,128)(2,1)}, f32[1376,768]{1,0:T(8,128)}) fusion(f32[768]{0:T(1024)S(1)} %reshape.223, bf16[768,768]{1,0:T(8,128)(2,1)} %all-gather.10.cloned.1.call-done, f32[1376,768]{1,0:T(8,128)} %subtract_multiply_fusion.1, f32[768]{0:T(1024)S(1)} %copy-done.41, f32[768]{0:T(1024)S(1)} %get-tuple-element.145), kind=kOutput, calls=%fused_computation.46 | convolution fusion | flops 1696112640 | bytes 11756544 | tf_op jit(solution)/shard_map/dot_general | solution.py:171
  255.8 5.7 fusion.72
  261.6 155.2 %all-reduce.6.cloned.1.call-done = f32[1376,768]{1,0:T(8,128)} async-done(((f32[1376,768]{1,0:T(8,128)}), f32[1376,768]{1,0:T(8,128)}) %all-reduce.6.cloned.1.call-update) | async-done | bytes 4227088 | tf_op jit(solution)/shard_map/psum | solution.py:174
  416.8 4.3 fusion.69
  423.2 1.3 fusion.66
  425.7 45.2 %all-gather.14.cloned.1.call-done = bf16[1376,768]{1,0:T(8,128)(2,1)} async-done(((bf16[344,768]{1,0:T(8,128)(2,1)}), bf16[1376,768]{1,0:T(8,128)(2,1)}) %all-gather.14.cloned.1.call-update) | async-done | bytes 2113552 | tf_op jit(solution)/shard_map/all_gather | solution.py:192
  470.8 5.2 convert_reduce_fusion
  476.1 1.4 copy-done.48
  477.4 3.9 fusion.73
  481.5 76.0 %reduce-scatter.12.cloned.1.call-done = f32[344,768]{1,0:T(8,128)} async-done(((f32[1376,768]{1,0:T(8,128)}), f32[344,768]{1,0:T(8,128)}) %reduce-scatter.12.cloned.1.call-update) | async-done | bytes 1056784 | tf_op jit(solution)/shard_map/reduce_scatter | solution.py:203
  557.5 2.0 multiply_reduce_fusion.4
  559.5 2.7 fusion.68
  562.3 5.7 fusion.74
  568.1 6.8 fusion.48
  575.3 33.8 %all-gather.16.cloned.1.call-done = bf16[1376,768]{1,0:T(8,128)(2,1)} async-done(((bf16[344,768]{1,0:T(8,128)(2,1)}), bf16[1376,768]{1,0:T(8,128)(2,1)}) %all-gather.16.cloned.1.call-update) | async-done | bytes 2113552 | tf_op jit(solution)/shard_map/all_gather | solution.py:208
  609.2 2.5 convolution_convert_fusion.3
  612.4 21.8 %while.25 = (s32[]{:T(128)}, bf16[2,688,192]{1,2,0:T(8,128)(2,1)S(1)}, bf16[2,688,576]{1,2,0:T(8,128)(2,1)}, bf16[2,688,3,3,64]{1,4,2,3,0:T(8,128)(2,1)S(1)}, f3...) while((s32[]{:T(128)}, bf16[2,688,192]{1,2,0:T(8,128)(2,1)S(1)}, ...), condition=%wide.region_17.18_spmd, body=%wide.region_15.17_spmd.sunk | while | flops 1113468160 | bytes 95243464 | solution.py:212
  613.6 1.1 convolution_convert_fusion.5
  614.8 1.2 fusion.118
  616.0 1.6 multiply_reduce_fusion.16
  617.6 1.5 multiply_convert_fusion.2
  621.3 1.2 copy-done.8
  624.6 1.1 convolution_convert_fusion.5
  625.8 1.2 fusion.118
  627.0 1.6 multiply_reduce_fusion.16
  628.5 1.5 multiply_convert_fusion.2
  632.2 1.2 copy-done.8
  635.3 2.2 convert_reduce_fusion.1
  638.5 3.5 convolution_bitcast_fusion
  642.2 3.9 copy.109
  646.1 5.0 fusion.44
  651.2 4.8 convolution_convert_fusion.2
  656.8 1.7 multiply_reduce_fusion.7
  658.5 1.7 multiply_reduce_fusion.8
  660.3 34.0 %reduce-scatter.24.cloned.1.call-done = f32[48,3]{1,0:T(8,128)} async-done(((f32[384,3]{1,0:T(8,128)}), f32[48,3]{1,0:T(8,128)}) %reduce-scatter.24.cloned.1.call-update) | async-done | bytes 592
  695.7 37.1 %reduce-scatter.22.cloned.1.call-done = f32[96,192]{1,0:T(8,128)} async-done(((f32[768,192]{1,0:T(8,128)}), f32[96,192]{1,0:T(8,128)}) %reduce-scatter.22.cloned.1.call-update) | async-done | bytes 73744
  734.4 42.2 %reduce-scatter.16.cloned.1.call-done = f32[96,576]{1,0:T(8,128)} async-done(((f32[768,576]{1,0:T(8,128)}), f32[96,576]{1,0:T(8,128)}) %reduce-scatter.16.cloned.1.call-update) | async-done | bytes 221200 | tf_op jit(solution)/shard_map/reduce_scatter | solution.py:244
  776.6 1.6 multiply_reduce_fusion.9
  781.5 41.2 %reduce-scatter.14.cloned.1.call-done = bf16[344,768]{1,0:T(8,128)(2,1)} async-done(((bf16[1376,768]{1,0:T(8,128)(2,1)}), bf16[344,768]{1,0:T(8,128)(2,1)}) %reduce-scatter.14.cloned.1.call-update) | async-done | bytes 528400 | tf_op jit(solution)/shard_map/reduce_scatter | solution.py:226
  822.7 2.2 fusion.59
  825.0 40.1 %all-reduce = (f32[]{:T(128)}, f32[7,768]{1,0:T(8,128)S(1)}) all-reduce(f32[]{:T(128)S(6)} %add.297, f32[7,768]{1,0:T(8,128)S(1)} %stack.59), channel_id=1, replica_groups=mesh['dp'=8,'mp'=4] {'dp','mp'}, use_global_device_ids=true, to_apply=%region_31.32 | all-reduce | flops 5377 | bytes 43016 | tf_op jit(solution)/shard_map/psum | solution.py:253
  867.2 1.3 multiply_subtract_fusion.5
  868.5 1.7 multiply_subtract_fusion.3
  870.2 1.4 multiply_subtract_fusion.4
  871.6 2.0 multiply_subtract_fusion.2
  (239 shorter events, 34.8 us)
Async XLA Ops:
  8.0 51.1 %all-gather.8.cloned.1.call-start = ((), (), s32[]{:S(2)}) async-start(), calls=%async_computation.7 | async-start | bytes 2641920 | tf_op jit(solution)/shard_map/all_gather | solution.py:146
  8.8 224.7 %all-reduce.4.cloned.1.call-start = ((), (), s32[]{:S(2)}) async-start(), calls=%async_computation.8 | async-start | bytes 8454144 | tf_op jit(solution)/shard_map/psum | solution.py:165
  9.5 12.6 %copy-start.37 = (pred[2,688]{1,0:T(4,128)(4,1)}, pred[2,688]{1,0:T(4,128)(4,1)S(1)}, u32[]{:S(2)}) copy-start(pred[2,688]{1,0:T(4,128)(4,1)S(1)} %broadcast_compare_fusion) | copy-start | bytes 4132
  9.6 49.5 %copy-start.34 = (pred[1376]{0:T(1024)(128)(4,1)}, pred[1376]{0:T(1024)(128)(4,1)S(1)}, u32[]{:S(2)}) copy-start(pred[1376]{0:T(1024)(128)(4,1)S(1)} %eq.23) | copy-start | bytes 4132
  43.3 196.2 %copy-start.32 = (f32[768]{0:T(1024)}, f32[768]{0:T(1024)S(1)}, u32[]{:S(2)}) copy-start(f32[768]{0:T(1024)S(1)} %get-tuple-element.147) | copy-start | bytes 9220
  54.4 4.8 copy-start.21
  65.0 10.5 %copy-start.10 = (bf16[192,768]{0,1:T(8,128)(2,1)S(1)}, bf16[192,768]{0,1:T(8,128)(2,1)}, u32[]{:S(2)}) copy-start(bf16[192,768]{0,1:T(8,128)(2,1)} %all_gather.35) | copy-start | bytes 884740
  78.3 1.7 copy-start.14
  78.3 2.6 copy-start.40
  78.3 155.2 %copy-start.35 = (pred[1376]{0:T(1024)(128)(4,1)S(1)}, pred[1376]{0:T(1024)(128)(4,1)}, u32[]{:S(2)}) copy-start(pred[1376]{0:T(1024)(128)(4,1)} %copy-done.34) | copy-start | bytes 4132
  78.3 163.9 %all-gather.10.cloned.1.call-start = ((), (), s32[]{:S(2)}) async-start(), calls=%async_computation.9 | async-start | bytes 1327104 | tf_op jit(solution)/shard_map/all_gather | solution.py:133
  79.9 175.9 %all-gather.12.cloned.1.call-start = ((), (), s32[]{:S(2)}) async-start(), calls=%async_computation.10 | async-start | bytes 1327104 | tf_op jit(solution)/shard_map/all_gather | solution.py:134
  80.7 336.1 %all-reduce.6.cloned.1.call-start = ((), (), s32[]{:S(2)}) async-start(), calls=%async_computation.11 | async-start | bytes 8454144 | tf_op jit(solution)/shard_map/psum | solution.py:174
  233.5 4.1 copy-start.2
  233.5 4.8 copy-start.3
  239.6 2.6 copy-start.41
  261.5 155.2 %copy-start.42 = (f32[768]{0:T(1024)S(1)}, f32[768]{0:T(1024)}, u32[]{:S(2)}) copy-start(f32[768]{0:T(1024)} %get-tuple-element.143) | copy-start | bytes 9220
  261.5 209.3 %all-gather.14.cloned.1.call-start = ((), (), s32[]{:S(2)}) async-start(), calls=%async_computation.12 | async-start | bytes 2641920 | tf_op jit(solution)/shard_map/all_gather | solution.py:192
  421.7 1.5 copy-start.44
  425.4 132.1 %reduce-scatter.12.cloned.1.call-start = ((), (), s32[]{:S(2)}) async-start(), calls=%async_computation.13 | async-start | bytes 5283840 | tf_op jit(solution)/shard_map/reduce_scatter | solution.py:203
  470.8 6.6 copy-start.47
  476.1 1.4 copy-start.48
  481.4 127.8 %all-gather.16.cloned.1.call-start = ((), (), s32[]{:S(2)}) async-start(), calls=%async_computation.14 | async-start | bytes 2641920 | tf_op jit(solution)/shard_map/all_gather | solution.py:208
  562.2 94.6 %reduce-scatter.20.cloned.1.call-start = ((), (), s32[]{:S(2)}) async-start(), calls=%async_computation.18 | async-start | bytes 2654208 | tf_op jit(solution)/shard_map/reduce_scatter | solution.py:247
  568.0 90.5 %reduce-scatter.18.cloned.1.call-start = ((), (), s32[]{:S(2)}) async-start(), calls=%async_computation.17 | async-start | bytes 2654208 | tf_op jit(solution)/shard_map/reduce_scatter | solution.py:246
  574.8 37.6 %copy-start.31 = (f32[2,3,688,1]{2,1,3,0:T(4,128)S(1)}, f32[2,3,688,1]{2,1,3,0:T(4,128)}, u32[]{:S(2)}) copy-start(f32[2,3,688,1]{2,1,3,0:T(4,128)} %get-tuple-element.312) | copy-start | bytes 49540
  574.9 119.4 %reduce-scatter.24.cloned.1.call-start = ((), (), s32[]{:S(2)}) async-start(), calls=%async_computation.20 | async-start | bytes 221184
  612.4 2.3 copy-start.5
  612.5 5.1 copy-start
  614.8 2.8 copy-start.11
  619.7 1.5 copy-start.7
  620.7 1.9 copy-start.1
  620.7 2.5 copy-start.6
  620.8 2.7 copy-start.12
  623.5 2.3 copy-start.5
  623.5 5.1 copy-start
  625.8 2.8 copy-start.11
  630.7 1.5 copy-start.7
  631.7 1.7 copy-start.1
  631.7 2.2 copy-start.6
  631.7 2.5 copy-start.12
  637.6 8.5 copy-start.4
  637.6 8.5 copy-start.33
  637.6 8.5 copy-start.36
  638.5 94.3 %reduce-scatter.22.cloned.1.call-start = ((), (), s32[]{:S(2)}) async-start(), calls=%async_computation.19 | async-start | bytes 884736
  642.0 134.6 %reduce-scatter.16.cloned.1.call-start = ((), (), s32[]{:S(2)}) async-start(), calls=%async_computation.16 | async-start | bytes 2211840 | tf_op jit(solution)/shard_map/reduce_scatter | solution.py:244
  646.1 5.1 copy-start.22
  651.1 4.9 copy-start.38
  651.1 171.6 %copy-start.9 = (f32[344,768]{1,0:T(8,128)S(1)}, f32[344,768]{1,0:T(8,128)}, u32[]{:S(2)}) copy-start(f32[344,768]{1,0:T(8,128)} %get-tuple-element.193) | copy-start | bytes 3170308
  651.1 171.6 %reduce-scatter.14.cloned.1.call-start = ((), (), s32[]{:S(2)}) async-start(), calls=%async_computation.15 | async-start | bytes 2641920 | tf_op jit(solution)/shard_map/reduce_scatter | solution.py:226
  656.0 211.2 %copy-start.45 = (f32[3,48]{1,0:T(4,128)S(1)}, f32[3,48]{1,0:T(4,128)}, u32[]{:S(2)}) copy-start(f32[3,48]{1,0:T(4,128)} %param.40) | copy-start | bytes 1732
  656.0 212.5 %copy-start.23 = (f32[192,96]{1,0:T(8,128)S(1)}, f32[192,96]{1,0:T(8,128)}, u32[]{:S(2)}) copy-start(f32[192,96]{1,0:T(8,128)} %param.31) | copy-start | bytes 221188
  656.0 214.2 %copy-start.43 = (f32[7,96]{1,0:T(8,128)S(1)}, f32[7,96]{1,0:T(8,128)}, u32[]{:S(2)}) copy-start(f32[7,96]{1,0:T(8,128)} %param.43) | copy-start | bytes 8068
  656.0 214.2 %copy-start.46 = (f32[7,96]{1,0:T(8,128)S(1)}, f32[7,96]{1,0:T(8,128)}, u32[]{:S(2)}) copy-start(f32[7,96]{1,0:T(8,128)} %param.44) | copy-start | bytes 8068
  656.0 215.6 %copy-start.20 = (f32[96,576]{1,0:T(8,128)S(1)}, f32[96,576]{1,0:T(8,128)}, u32[]{:S(2)}) copy-start(f32[96,576]{1,0:T(8,128)} %param.28) | copy-start | bytes 663556
  656.0 215.6 %copy-start.28 = (f32[96,576]{1,0:T(8,128)S(1)}, f32[96,576]{1,0:T(8,128)}, u32[]{:S(2)}) copy-start(f32[96,576]{1,0:T(8,128)} %param.29) | copy-start | bytes 663556
  656.0 217.6 %copy-start.15 = (f32[768,96]{0,1:T(8,128)S(1)}, f32[768,96]{0,1:T(8,128)}, u32[]{:S(2)}) copy-start(f32[768,96]{0,1:T(8,128)} %param.37) | copy-start | bytes 884740
  656.0 217.6 %copy-start.24 = (f32[768,96]{0,1:T(8,128)S(1)}, f32[768,96]{0,1:T(8,128)}, u32[]{:S(2)}) copy-start(f32[768,96]{0,1:T(8,128)} %param.38) | copy-start | bytes 884740
  656.0 217.6 %copy-start.25 = (f32[768,96]{0,1:T(8,128)S(1)}, f32[768,96]{0,1:T(8,128)}, u32[]{:S(2)}) copy-start(f32[768,96]{0,1:T(8,128)} %param.39) | copy-start | bytes 884740
  656.8 217.9 %copy-start.17 = (f32[96,768]{1,0:T(8,128)S(1)}, f32[96,768]{1,0:T(8,128)}, u32[]{:S(2)}) copy-start(f32[96,768]{1,0:T(8,128)} %param.34) | copy-start | bytes 884740
  656.8 216.8 %copy-start.18 = (f32[768,96]{0,1:T(8,128)S(1)}, f32[768,96]{0,1:T(8,128)}, u32[]{:S(2)}) copy-start(f32[768,96]{0,1:T(8,128)} %reduce-scatter.20.cloned.1.call-done) | copy-start | bytes 884740
  658.5 216.2 %copy-start.19 = (f32[96,768]{1,0:T(8,128)S(1)}, f32[96,768]{1,0:T(8,128)}, u32[]{:S(2)}) copy-start(f32[96,768]{1,0:T(8,128)} %reduce-scatter.18.cloned.1.call-done) | copy-start | bytes 884740
  825.0 49.7 %copy-start.26 = (f32[96,768]{1,0:T(8,128)S(1)}, f32[96,768]{1,0:T(8,128)}, u32[]{:S(2)}) copy-start(f32[96,768]{1,0:T(8,128)} %param.35) | copy-start | bytes 884740
  825.0 49.7 %copy-start.27 = (f32[96,768]{1,0:T(8,128)S(1)}, f32[96,768]{1,0:T(8,128)}, u32[]{:S(2)}) copy-start(f32[96,768]{1,0:T(8,128)} %param.36) | copy-start | bytes 884740
  (9 other events, 9.6 us)
Sparse Core Ops, SparseCore 0:
  10.4 48.6 all-gather.7
  78.4 155.0 all-reduce.3
  261.7 155.0 all-reduce.5
  425.5 45.2 all-gather.13
  481.5 75.9 reduce-scatter.11
  562.3 46.7 all-gather.15
Sparse Core Ops, SparseCore 1:
  81.2 22.9 all-gather.9
  106.5 23.9 all-gather.11
  568.1 42.9 reduce-scatter.19
  614.7 42.4 reduce-scatter.17
  660.8 33.5 reduce-scatter.23
  697.8 34.9 reduce-scatter.21
  736.4 40.1 reduce-scatter.15
  778.8 43.9 reduce-scatter.13
where the time goes:
time: 894 us; the launch traced here: 885 us
  waiting for transfers between devices  623 us (70%)
  matrix products  80.1 us (9%)
  blocking collectives  80 us (9%)
  other arithmetic  50.3 us (6%)
  local copies, waits for them, and re-layouts  26.9 us (3%)
  between operations  22.1 us (2%)
    psum x1, waiting for transfers between devices, on_device(): second_sum = hidden + lax.psum(ffn_part, 'mp') + vectors[6]  155 us
    psum x1, waiting for transfers between devices, on_device(): attended = lax.psum(attn_part, 'mp')  153 us
    reduce_scatter x1, waiting for transfers between devices, on_device(): lax.psum_scatter(hidden_part, 'mp', scatter_dimension=0, tiled=True)  76 us
    unnamed x16, waiting for transfers between devices  72 us
    all_gather x1, waiting for transfers between devices, on_device(): lax.all_gather(grad_two.astype(jnp.bfloat16), 'mp', axis=0, tiled=True)  45.2 us
    reduce_scatter x1, waiting for transfers between devices, on_device(): lax.psum_scatter(grad_qkv, 'dp', scatter_dimension=0, tiled=True)  42.2 us
    reduce_scatter x1, waiting for transfers between devices, on_device(): lax.psum_scatter(input_part.astype(jnp.bfloat16), 'mp', scatter_dimension...  41.2 us
    psum x1, blocking collectives, on_device(): lax.psum((local_squares, grad_vectors), ('dp', 'mp'))  40.1 us
  transfers between devices with their start and end apart: 14, of which 10 were waited for; matrix products, arithmetic and copies ran while one was open for 10% of the time, Pallas kernels for 0%

commit v1 on v0

--- a/solution.py
+++ b/solution.py
@@ -171,7 +171,7 @@
     pre_act = jnp.dot(hidden_low, up_full, preferred_element_type=jnp.float32) + up_bias
     activated = jax.nn.gelu(pre_act, approximate=False).astype(jnp.bfloat16)
     ffn_part = jnp.dot(activated, down_full, preferred_element_type=jnp.float32)
-    second_sum = hidden + lax.psum(ffn_part, "mp") + vectors[6]
+    second_sum = hidden + jnp.sum(lax.all_gather(ffn_part, axis_name="mp"), axis=0) + vectors[6]
     outputs_full, normed_full, inverse_full = norm_rows(second_sum, vectors[3], vectors[4])
     outputs = share_of(outputs_full)
     normed_two = share_of(normed_full)

time: 894 us -> 1040 us (1.16)
  waiting for transfers between devices: 623 us -> 756 us
    all_gather x0 -> x1, waiting for transfers between devices: none -> 289 us  [on_device(): lax.all_gather(ffn_part, axis_name='mp')]
    psum x1 -> x0, waiting for transfers between devices: 155 us -> none  [on_device(): second_sum = hidden + lax.psum(ffn_part, 'mp') + vectors[6]]
  transfers between devices with their start and end apart: 14 -> 14, of which waited for: 10 -> 10; matrix products, arithmetic and copies ran while one was open for 10% -> 9% of each run, Pallas kernels for 0% -> 0%
where the time goes in v1:
time: 1040 us; the launch traced here: 1030 us
  waiting for transfers between devices  756 us (73%)
  matrix products  81 us (8%)
  blocking collectives  80 us (8%)
  other arithmetic  59.6 us (6%)
  local copies, waits for them, and re-layouts  28.2 us (3%)
  between operations  22.1 us (2%)
    all_gather x1, waiting for transfers between devices, on_device(): lax.all_gather(ffn_part, axis_name='mp')  289 us
    psum x1, waiting for transfers between devices, on_device(): attended = lax.psum(attn_part, 'mp')  152 us
    reduce_scatter x1, waiting for transfers between devices, on_device(): lax.psum_scatter(hidden_part, 'mp', scatter_dimension=0, tiled=True)  76.1 us
    unnamed x16, waiting for transfers between devices  70.5 us
    all_gather x1, waiting for transfers between devices, on_device(): lax.all_gather(grad_two.astype(jnp.bfloat16), 'mp', axis=0, tiled=True)  45.5 us
    reduce_scatter x1, waiting for transfers between devices, on_device(): lax.psum_scatter(grad_qkv, 'dp', scatter_dimension=0, tiled=True)  42.3 us
    reduce_scatter x1, waiting for transfers between devices, on_device(): lax.psum_scatter(input_part.astype(jnp.bfloat16), 'mp', scatter_dimension...  41.2 us
    psum x1, blocking collectives, on_device(): lax.psum((local_squares, grad_vectors), ('dp', 'mp'))  40.1 us
  transfers between devices with their start and end apart: 14, of which 10 were waited for; matrix products, arithmetic and copies ran while one was open for 9% of the time, Pallas kernels for 0%

profile of v1, /device:TPU:0, one launch (start us, length us, event | category | flops | bytes accessed | tf_op | source)
XLA Modules:
  0.0 1029.1 jit_solution(10268861368586029242)
XLA Ops:
  9.5 10.3 %all-gather.1 = bf16[8,96,7]{1,2,0:T(8,128)(2,1)S(1)} all-gather(bf16[1,96,7]{1,2,0:T(8,128)(2,1)S(1)} %convert_bitcast_fusion), channel_id=1, replica_groups=mesh['dp'=8,'mp'=4] {'dp'}, dimensions={0}, use_global_device_ids=true | all-gather | bytes 12096 | tf_op jit(solution)/shard_map/all_gather | solution.py:136
  21.4 8.9 all-gather.2
  33.1 9.6 all_gather.41
  43.3 11.0 %all_gather.39 = bf16[768,576]{1,0:T(8,128)(2,1)S(1)} all-gather(bf16[96,576]{1,0:T(8,128)(2,1)S(1)} %convert_element_type.121), channel_id=1, replica_groups=mesh['dp'=8,'mp'=4] {'dp'}, dimensions={0}, use_global_device_ids=true | all-gather | bytes 995328 | tf_op jit(solution)/shard_map/all_gather | solution.py:131
  54.4 5.0 all-gather.10.cloned.1.call-done
  59.4 3.4 fusion.36
  62.8 2.1 reshape.215
  65.3 7.0 while.24
  67.6 1.1 fusion.110
  71.0 1.1 fusion.110
  72.2 1.4 copy.105
  73.6 2.1 reshape.216
  75.7 2.8 fusion.71
  81.2 152.3 %all-reduce.3.cloned.1.call-done = f32[1376,768]{1,0:T(8,128)} async-done(((f32[1376,768]{1,0:T(8,128)}), f32[1376,768]{1,0:T(8,128)}) %all-reduce.3.cloned.1.call-update) | async-done | bytes 4227088 | tf_op jit(solution)/shard_map/psum | solution.py:165
  233.5 4.0 fusion.58
  238.3 1.3 multiply_reduce_fusion.3
  239.6 2.6 subtract_multiply_fusion.1
  242.2 13.6 %fusion.20 = (bf16[1376,768]{1,0:T(8,128)(2,1)}, f32[1376,768]{1,0:T(8,128)}) fusion(f32[768]{0:T(1024)S(1)} %reshape.223, bf16[768,768]{1,0:T(8,128)(2,1)} %all-gather.12.cloned.1.call-done, f32[1376,768]{1,0:T(8,128)} %subtract_multiply_fusion.1, f32[768]{0:T(1024)S(1)} %copy-done.39, f32[768]{0:T(1024)S(1)} %get-tuple-element.145), kind=kOutput, calls=%fused_computation.46 | convolution fusion | flops 1696112640 | bytes 11756544 | tf_op jit(solution)/shard_map/dot_general | solution.py:171
  255.8 5.7 fusion.72
  261.8 289.4 %all-gather.20.cloned.1.call-done = f32[5504,768]{1,0:T(8,128)} async-done(((f32[1376,768]{1,0:T(8,128)}), f32[5504,768]{1,0:T(8,128)}) %all-gather.20.cloned.1.call-update) | async-done | bytes 16908304 | tf_op jit(solution)/shard_map/all_gather | solution.py:174
  551.2 9.4 reduce_sum.236
  560.7 4.3 fusion.69
  567.1 1.3 fusion.66
  569.4 45.5 %all-gather.16.cloned.1.call-done = bf16[1376,768]{1,0:T(8,128)(2,1)} async-done(((bf16[344,768]{1,0:T(8,128)(2,1)}), bf16[1376,768]{1,0:T(8,128)(2,1)}) %all-gather.16.cloned.1.call-update) | async-done | bytes 2113552 | tf_op jit(solution)/shard_map/all_gather | solution.py:192
  614.8 5.2 convert_reduce_fusion
  620.1 1.3 copy-done.46
  621.4 3.8 fusion.73
  625.4 76.1 %reduce-scatter.12.cloned.1.call-done = f32[344,768]{1,0:T(8,128)} async-done(((f32[1376,768]{1,0:T(8,128)}), f32[344,768]{1,0:T(8,128)}) %reduce-scatter.12.cloned.1.call-update) | async-done | bytes 1056784 | tf_op jit(solution)/shard_map/reduce_scatter | solution.py:203
  701.5 2.0 multiply_reduce_fusion.4
  703.5 2.7 fusion.68
  706.2 6.4 fusion.48
  712.7 5.9 fusion.74
  719.1 34.0 %all-gather.18.cloned.1.call-done = bf16[1376,768]{1,0:T(8,128)(2,1)} async-done(((bf16[344,768]{1,0:T(8,128)(2,1)}), bf16[1376,768]{1,0:T(8,128)(2,1)}) %all-gather.18.cloned.1.call-update) | async-done | bytes 2113552 | tf_op jit(solution)/shard_map/all_gather | solution.py:208
  753.1 3.3 convolution_convert_fusion.3
  756.4 2.4 reshape.217
  758.9 21.4 %while.25 = (s32[]{:T(128)}, bf16[2,688,192]{1,2,0:T(8,128)(2,1)S(1)}, bf16[2,688,576]{1,2,0:T(8,128)(2,1)}, bf16[2,688,3,3,64]{1,4,2,3,0:T(8,128)(2,1)S(1)}, f3...) while((s32[]{:T(128)}, bf16[2,688,192]{1,2,0:T(8,128)(2,1)S(1)}, ...), condition=%wide.region_17.18_spmd, body=%wide.region_15.17_spmd.sunk | while | flops 1113468160 | bytes 91016328 | solution.py:212
  760.0 1.1 convolution_convert_fusion.5
  761.3 1.6 multiply_reduce_fusion.16
  762.9 1.5 multiply_convert_fusion.2
  766.0 1.2 fusion.118
  767.7 1.2 copy-done.6
  770.8 1.1 convolution_convert_fusion.5
  772.0 1.6 multiply_reduce_fusion.16
  773.6 1.5 multiply_convert_fusion.2
  776.8 1.2 fusion.118
  778.3 1.2 copy-done.6
  780.3 1.9 convert_reduce_fusion.1
  784.3 3.6 convolution_bitcast_fusion
  788.2 3.9 copy.109
  792.1 5.0 fusion.44
  797.2 4.8 convolution_convert_fusion.2
  802.9 1.7 multiply_reduce_fusion.8
  804.6 1.7 multiply_reduce_fusion.7
  806.3 32.6 %reduce-scatter.24.cloned.1.call-done = f32[48,3]{1,0:T(8,128)} async-done(((f32[384,3]{1,0:T(8,128)}), f32[48,3]{1,0:T(8,128)}) %reduce-scatter.24.cloned.1.call-update) | async-done | bytes 592
  840.3 37.1 %reduce-scatter.22.cloned.1.call-done = f32[96,192]{1,0:T(8,128)} async-done(((f32[768,192]{1,0:T(8,128)}), f32[96,192]{1,0:T(8,128)}) %reduce-scatter.22.cloned.1.call-update) | async-done | bytes 73744
  879.0 42.3 %reduce-scatter.16.cloned.1.call-done = f32[96,576]{1,0:T(8,128)} async-done(((f32[768,576]{1,0:T(8,128)}), f32[96,576]{1,0:T(8,128)}) %reduce-scatter.16.cloned.1.call-update) | async-done | bytes 221200 | tf_op jit(solution)/shard_map/reduce_scatter | solution.py:244
  921.2 1.7 multiply_reduce_fusion.9
  926.1 41.2 %reduce-scatter.14.cloned.1.call-done = bf16[344,768]{1,0:T(8,128)(2,1)} async-done(((bf16[1376,768]{1,0:T(8,128)(2,1)}), bf16[344,768]{1,0:T(8,128)(2,1)}) %reduce-scatter.14.cloned.1.call-update) | async-done | bytes 528400 | tf_op jit(solution)/shard_map/reduce_scatter | solution.py:226
  967.3 2.2 fusion.59
  969.6 40.1 %all-reduce = (f32[]{:T(128)}, f32[7,768]{1,0:T(8,128)S(1)}) all-reduce(f32[]{:T(128)S(6)} %add.295, f32[7,768]{1,0:T(8,128)S(1)} %stack.59), channel_id=1, replica_groups=mesh['dp'=8,'mp'=4] {'dp','mp'}, use_global_device_ids=true, to_apply=%region_31.32 | all-reduce | flops 5377 | bytes 43016 | tf_op jit(solution)/shard_map/psum | solution.py:253
  1011.7 1.3 multiply_subtract_fusion.5
  1013.0 1.7 multiply_subtract_fusion.3
  1014.7 1.4 multiply_subtract_fusion.4
  1017.2 2.1 multiply_subtract_fusion.1
  (232 shorter events, 35.8 us)
Async XLA Ops:
  8.0 51.4 %all-gather.10.cloned.1.call-start = ((), (), s32[]{:S(2)}) async-start(), calls=%async_computation.7 | async-start | bytes 2641920 | tf_op jit(solution)/shard_map/all_gather | solution.py:146
  8.8 224.7 %all-reduce.3.cloned.1.call-start = ((), (), s32[]{:S(2)}) async-start(), calls=%async_computation.8 | async-start | bytes 8454144 | tf_op jit(solution)/shard_map/psum | solution.py:165
  20.6 10.4 %copy-start.35 = (pred[2,688]{1,0:T(4,128)(4,1)}, pred[2,688]{1,0:T(4,128)(4,1)S(1)}, u32[]{:S(2)}) copy-start(pred[2,688]{1,0:T(4,128)(4,1)S(1)} %broadcast_compare_fusion) | copy-start | bytes 4132
  20.7 38.7 %copy-start.32 = (pred[1376]{0:T(1024)(128)(4,1)}, pred[1376]{0:T(1024)(128)(4,1)S(1)}, u32[]{:S(2)}) copy-start(pred[1376]{0:T(1024)(128)(4,1)S(1)} %eq.23) | copy-start | bytes 4132
  43.3 196.2 %copy-start.30 = (f32[768]{0:T(1024)}, f32[768]{0:T(1024)S(1)}, u32[]{:S(2)}) copy-start(f32[768]{0:T(1024)S(1)} %get-tuple-element.147) | copy-start | bytes 9220
  54.4 5.0 copy-start.20
  65.3 10.5 %copy-start.8 = (bf16[192,768]{0,1:T(8,128)(2,1)S(1)}, bf16[192,768]{0,1:T(8,128)(2,1)}, u32[]{:S(2)}) copy-start(bf16[192,768]{0,1:T(8,128)(2,1)} %all_gather.41) | copy-start | bytes 884740
  67.5 1.2 copy-start.28
  71.0 1.2 copy-start.28
  78.5 1.7 copy-start.12
  78.5 2.6 copy-start.38
  78.5 155.0 %copy-start.33 = (pred[1376]{0:T(1024)(128)(4,1)S(1)}, pred[1376]{0:T(1024)(128)(4,1)}, u32[]{:S(2)}) copy-start(pred[1376]{0:T(1024)(128)(4,1)} %copy-done.32) | copy-start | bytes 4132
  78.6 163.6 %all-gather.12.cloned.1.call-start = ((), (), s32[]{:S(2)}) async-start(), calls=%async_computation.9 | async-start | bytes 1327104 | tf_op jit(solution)/shard_map/all_gather | solution.py:133
  80.2 175.6 %all-gather.14.cloned.1.call-start = ((), (), s32[]{:S(2)}) async-start(), calls=%async_computation.10 | async-start | bytes 1327104 | tf_op jit(solution)/shard_map/all_gather | solution.py:134
  81.0 470.3 %all-gather.20.cloned.1.call-start = ((), (), s32[]{:S(2)}) async-start(), calls=%async_computation.18 | async-start | bytes 21135360 | tf_op jit(solution)/shard_map/all_gather | solution.py:174
  233.5 4.1 copy-start.2
  233.5 4.8 copy-start.3
  239.6 2.6 copy-start.39
  261.6 353.3 %all-gather.16.cloned.1.call-start = ((), (), s32[]{:S(2)}) async-start(), calls=%async_computation.11 | async-start | bytes 2641920 | tf_op jit(solution)/shard_map/all_gather | solution.py:192
  551.2 9.4 copy-start.40
  565.7 1.5 copy-start.42
  569.3 132.1 %reduce-scatter.12.cloned.1.call-start = ((), (), s32[]{:S(2)}) async-start(), calls=%async_computation.12 | async-start | bytes 5283840 | tf_op jit(solution)/shard_map/reduce_scatter | solution.py:203
  614.8 6.6 copy-start.45
  620.1 1.3 copy-start.46
  625.3 127.8 %all-gather.18.cloned.1.call-start = ((), (), s32[]{:S(2)}) async-start(), calls=%async_computation.13 | async-start | bytes 2641920 | tf_op jit(solution)/shard_map/all_gather | solution.py:208
  706.2 96.7 %reduce-scatter.18.cloned.1.call-start = ((), (), s32[]{:S(2)}) async-start(), calls=%async_computation.16 | async-start | bytes 2654208 | tf_op jit(solution)/shard_map/reduce_scatter | solution.py:246
  712.6 92.0 %reduce-scatter.20.cloned.1.call-start = ((), (), s32[]{:S(2)}) async-start(), calls=%async_computation.17 | async-start | bytes 2654208 | tf_op jit(solution)/shard_map/reduce_scatter | solution.py:247
  718.6 40.3 %copy-start.29 = (f32[2,3,688,1]{2,1,3,0:T(4,128)S(1)}, f32[2,3,688,1]{2,1,3,0:T(4,128)}, u32[]{:S(2)}) copy-start(f32[2,3,688,1]{2,1,3,0:T(4,128)} %get-tuple-element.312) | copy-start | bytes 49540
  718.6 120.2 %reduce-scatter.24.cloned.1.call-start = ((), (), s32[]{:S(2)}) async-start(), calls=%async_computation.20 | async-start | bytes 221184
  758.9 3.9 copy-start
  761.3 1.6 copy-start.9
  766.0 1.6 copy-start.5
  767.2 1.9 copy-start.1
  767.2 2.5 copy-start.10
  767.7 1.2 copy-start.6
  769.7 3.9 copy-start
  772.0 1.6 copy-start.9
  776.8 1.5 copy-start.5
  777.9 1.9 copy-start.1
  777.9 2.3 copy-start.10
  778.3 1.2 copy-start.6
  784.2 7.9 copy-start.4
  784.2 7.9 copy-start.31
  784.2 7.9 copy-start.34
  784.3 93.1 %reduce-scatter.22.cloned.1.call-start = ((), (), s32[]{:S(2)}) async-start(), calls=%async_computation.19 | async-start | bytes 884736
  787.9 133.3 %reduce-scatter.16.cloned.1.call-start = ((), (), s32[]{:S(2)}) async-start(), calls=%async_computation.15 | async-start | bytes 2211840 | tf_op jit(solution)/shard_map/reduce_scatter | solution.py:244
  792.1 5.1 copy-start.21
  797.1 4.9 copy-start.36
  797.2 170.2 %copy-start.7 = (f32[344,768]{1,0:T(8,128)S(1)}, f32[344,768]{1,0:T(8,128)}, u32[]{:S(2)}) copy-start(f32[344,768]{1,0:T(8,128)} %get-tuple-element.193) | copy-start | bytes 3170308
  797.2 170.1 %reduce-scatter.14.cloned.1.call-start = ((), (), s32[]{:S(2)}) async-start(), calls=%async_computation.14 | async-start | bytes 2641920 | tf_op jit(solution)/shard_map/reduce_scatter | solution.py:226
  802.0 209.7 %copy-start.43 = (f32[3,48]{1,0:T(4,128)S(1)}, f32[3,48]{1,0:T(4,128)}, u32[]{:S(2)}) copy-start(f32[3,48]{1,0:T(4,128)} %param.40) | copy-start | bytes 1732
  802.0 211.0 %copy-start.22 = (f32[192,96]{1,0:T(8,128)S(1)}, f32[192,96]{1,0:T(8,128)}, u32[]{:S(2)}) copy-start(f32[192,96]{1,0:T(8,128)} %param.31) | copy-start | bytes 221188
  802.0 212.7 %copy-start.41 = (f32[7,96]{1,0:T(8,128)S(1)}, f32[7,96]{1,0:T(8,128)}, u32[]{:S(2)}) copy-start(f32[7,96]{1,0:T(8,128)} %param.43) | copy-start | bytes 8068
  802.0 212.7 %copy-start.44 = (f32[7,96]{1,0:T(8,128)S(1)}, f32[7,96]{1,0:T(8,128)}, u32[]{:S(2)}) copy-start(f32[7,96]{1,0:T(8,128)} %param.44) | copy-start | bytes 8068
  802.0 214.1 %copy-start.13 = (f32[768,96]{0,1:T(8,128)S(1)}, f32[768,96]{0,1:T(8,128)}, u32[]{:S(2)}) copy-start(f32[768,96]{0,1:T(8,128)} %param.37) | copy-start | bytes 884740
  802.0 214.1 %copy-start.23 = (f32[768,96]{0,1:T(8,128)S(1)}, f32[768,96]{0,1:T(8,128)}, u32[]{:S(2)}) copy-start(f32[768,96]{0,1:T(8,128)} %param.38) | copy-start | bytes 884740
  802.0 214.1 %copy-start.24 = (f32[768,96]{0,1:T(8,128)S(1)}, f32[768,96]{0,1:T(8,128)}, u32[]{:S(2)}) copy-start(f32[768,96]{0,1:T(8,128)} %param.39) | copy-start | bytes 884740
  802.1 215.1 %copy-start.15 = (f32[96,768]{1,0:T(8,128)S(1)}, f32[96,768]{1,0:T(8,128)}, u32[]{:S(2)}) copy-start(f32[96,768]{1,0:T(8,128)} %param.34) | copy-start | bytes 884740
  802.8 214.4 %copy-start.16 = (f32[96,768]{1,0:T(8,128)S(1)}, f32[96,768]{1,0:T(8,128)}, u32[]{:S(2)}) copy-start(f32[96,768]{1,0:T(8,128)} %reduce-scatter.18.cloned.1.call-done) | copy-start | bytes 884740
  804.6 214.8 %copy-start.18 = (f32[96,576]{1,0:T(8,128)S(1)}, f32[96,576]{1,0:T(8,128)}, u32[]{:S(2)}) copy-start(f32[96,576]{1,0:T(8,128)} %param.28) | copy-start | bytes 663556
  804.6 211.6 %copy-start.17 = (f32[768,96]{0,1:T(8,128)S(1)}, f32[768,96]{0,1:T(8,128)}, u32[]{:S(2)}) copy-start(f32[768,96]{0,1:T(8,128)} %reduce-scatter.20.cloned.1.call-done) | copy-start | bytes 884740
  921.2 98.1 %copy-start.19 = (f32[96,576]{1,0:T(8,128)S(1)}, f32[96,576]{1,0:T(8,128)}, u32[]{:S(2)}) copy-start(f32[96,576]{1,0:T(8,128)} %reduce-scatter.16.cloned.1.call-done) | copy-start | bytes 663556
  969.6 49.8 %copy-start.25 = (f32[96,576]{1,0:T(8,128)S(1)}, f32[96,576]{1,0:T(8,128)}, u32[]{:S(2)}) copy-start(f32[96,576]{1,0:T(8,128)} %param.29) | copy-start | bytes 663556
  969.6 49.8 %copy-start.26 = (f32[96,576]{1,0:T(8,128)S(1)}, f32[96,576]{1,0:T(8,128)}, u32[]{:S(2)}) copy-start(f32[96,576]{1,0:T(8,128)} %param.30) | copy-start | bytes 663556
  (5 other events, 4.8 us)
Sparse Core Ops, SparseCore 0:
  10.4 48.9 all-gather.9
  78.7 154.7 all-reduce.2
  261.7 289.4 all-gather.19
  569.5 45.3 all-gather.15
  625.4 76.0 reduce-scatter.11
  706.3 46.7 all-gather.17
Sparse Core Ops, SparseCore 1:
  81.5 22.6 all-gather.11
  106.5 23.9 all-gather.13
  712.7 42.8 reduce-scatter.17
  759.3 42.3 reduce-scatter.19
  805.3 33.6 reduce-scatter.23
  842.3 34.9 reduce-scatter.21
  881.0 40.2 reduce-scatter.15
  923.4 43.9 reduce-scatter.13
